TPU v7x, 32 devices: a whole 2x2x4 slice. The times are simulated.
32 devices in a mesh: row: 4 (over y, x), col: 8 (over z, core).
Axes of the slice: x: 2, y: 2, z: 4, core: 2. Of those that a mesh axis runs over, the one named last changes fastest.
Arguments:
- images: float32 [64, 28, 28, 3], P(('row', 'col')), may hold values from -6 to 6
- noise_field: float32 [64, 28, 28, 3], P(('row', 'col')), may hold values from -6 to 6
- stem_weight: bfloat16 [27, 256], replicated, may hold values from -1.25 to 1.25
- level_one: bfloat16 [4, 2304, 256], replicated, may hold values from -0.125 to 0.125
- down_weight: bfloat16 [1024, 256], replicated, may hold values from -0.1875 to 0.1875
- level_two: bfloat16 [2, 2304, 256], replicated, may hold values from -0.125 to 0.125
- up_weight: bfloat16 [256, 1024], replicated, may hold values from -0.375 to 0.375
- out_weight: bfloat16 [256, 3], replicated, may hold values from -0.375 to 0.375
- embed_weight: bfloat16 [588, 6144], replicated
- embed_bias: float32 [6144], replicated
- mlp_in: bfloat16 [6144, 24576], P('col', 'row'), may hold values from -0.078125 to 0.078125
- mlp_out: bfloat16 [24576, 6144], P('row', 'col'), may hold values from -0.0390625 to 0.0390625
Outputs:
- purified: float32 [64, 28, 28, 3], P(('row', 'col'))
- encoded: bfloat16 [256, 6144], P('row', 'col')
All inputs are finite; a program needn't handle non-finite values.
Results may differ from a plain program's by a relative error of at most 0.018.
Values may be sent and summed in bfloat16 or wider, within the bound.
A program may use at most 128 MiB of HBM per device.

v0:
```python
import functools
import math

import jax
import jax.numpy as jnp
from jax import lax
from jax.experimental import pallas as pl
from jax.experimental.pallas import tpu as pltpu
from jax.sharding import PartitionSpec as P

PATCH = 14
SIDE = 28
WIDE = 32
HALF = 14
HWIDE = 16

step_size = 0.25
noise_gain = math.sqrt(0.5)
ln_epsilon = 1e-06
MESH = pl.DeviceIdType.MESH
MIB = 1024 * 1024
f32 = jnp.float32
bf16 = jnp.bfloat16


def dot(a, b):
    return jnp.dot(a, b, preferred_element_type=f32)


def remote(src, dst, send_sem, recv_sem, device):
    return pltpu.make_async_remote_copy(
        src_ref=src,
        dst_ref=dst,
        send_sem=send_sem,
        recv_sem=recv_sem,
        device_id=device,
        device_id_type=MESH,
    )


def masked_act(stream, wide, side):
    column = lax.broadcasted_iota(jnp.int32, stream.shape, 0) % wide
    return jnp.where(column < side, jax.nn.gelu(stream), 0.0)


def put_act(field, at, stream, wide, side):
    depth = stream.shape[1]
    rows = stream.shape[0]
    act = masked_act(stream, wide, side)
    field[pl.ds(at, rows), 0:depth] = pltpu.roll(act, 1, 0).astype(bf16)
    field[pl.ds(at, rows), depth : 2 * depth] = act.astype(bf16)
    field[pl.ds(at, rows), 2 * depth : 3 * depth] = pltpu.roll(act, rows - 1, 0).astype(bf16)


def conv_rows(field, weight, at, rows, wide):
    span = weight.shape[0] // 3
    total = None
    for row_off in range(3):
        part = dot(
            field[at + row_off * wide : at + row_off * wide + rows, :],
            weight[row_off * span : (row_off + 1) * span, :],
        )
        total = part if total is None else total + part
    return total


def score_kernel(
    pixels,
    noise,
    stem,
    level_one,
    down,
    level_two,
    up,
    out_t,
    mlp_in,
    mlp_out,
    purified,
    in_swapped,
    out_swapped,
    field_a,
    field_b,
    coarse_a,
    coarse_b,
    stream,
    halves,
    coarse,
    send_sem,
    recv_sem,
):
    col = lax.axis_index("col")
    core = col % 2
    sibling = {"col": col + 1 - 2 * core}
    barrier = pltpu.get_barrier_semaphore()
    pl.semaphore_signal(barrier, inc=1, device_id=sibling, device_id_type=MESH)
    pl.semaphore_wait(barrier, 1)
    width = mlp_in.shape[1] // 2
    height = mlp_out.shape[0] // 2
    swaps = [
        remote(
            mlp_in.at[:, pl.ds(pl.multiple_of((1 - core) * width, 128), width)],
            in_swapped,
            send_sem.at[0],
            recv_sem.at[0],
            sibling,
        ),
        remote(
            mlp_out.at[pl.ds(pl.multiple_of((1 - core) * height, 16), height), :],
            out_swapped,
            send_sem.at[1],
            recv_sem.at[1],
            sibling,
        ),
    ]
    for swap in swaps:
        swap.start()

    depth = stream.shape[1]
    cells = SIDE * WIDE
    ccells = HALF * HWIDE
    tile = 7 * WIDE
    for field, row, last in (
        (field_a, WIDE, cells),
        (field_b, WIDE, cells),
        (coarse_a, HWIDE, ccells),
        (coarse_b, HWIDE, ccells),
    ):
        field[0:row, :] = jnp.zeros((row, 3 * depth), bf16)
        field[row + last : row + last + row, :] = jnp.zeros((row, 3 * depth), bf16)

    def one_image(n, carry):
        view = pixels[n].astype(bf16).astype(f32)
        lanes = view.shape[1]
        groups = []
        for row_off in (-1, 0, 1):
            for col_off in (-1, 0, 1):
                shift = (-(row_off * WIDE + col_off)) % lanes
                groups.append(pltpu.roll(view, shift, 1) if shift else view)
        groups.extend([jnp.zeros_like(view)] * 7)
        columns = jnp.concatenate(groups, axis=0).T.astype(bf16)
        for at in range(0, cells, tile):
            now = dot(columns[at : at + tile, :], stem[...])
            stream[at : at + tile, :] = now
            put_act(field_a, WIDE + at, now, WIDE, SIDE)
        for at in range(0, cells, tile):
            now = stream[at : at + tile, :] + conv_rows(
                field_a, level_one.at[0], at, tile, WIDE
            )
            stream[at : at + tile, :] = now
            put_act(field_b, WIDE + at, now, WIDE, SIDE)
        for at in range(0, cells, tile):
            now = stream[at : at + tile, :] + conv_rows(
                field_b, level_one.at[1], at, tile, WIDE
            )
            stream[at : at + tile, :] = now
            for h in range(depth // 128):
                stream_halves[h][at : at + tile, :] = now[:, h * 128 : (h + 1) * 128]
        now = None
        for b in range(2):
            parts = [
                half[pl.ds(b, cells // 2, stride=2), :].astype(bf16).reshape(HALF, 2, HWIDE, 128)
                for half in stream_halves
            ]
            for a in range(2):
                piece = jnp.concatenate(
                    [part[:, a].reshape(ccells, 128) for part in parts], axis=1
                )
                at = (2 * a + b) * depth
                part = dot(piece, down[at : at + depth, :])
                now = part if now is None else now + part
        put_act(coarse_a, HWIDE, now, HWIDE, HALF)
        now = now + conv_rows(coarse_a, level_two.at[0], 0, ccells, HWIDE)
        put_act(coarse_b, HWIDE, now, HWIDE, HALF)
        now = now + conv_rows(coarse_b, level_two.at[1], 0, ccells, HWIDE)
        lifted = now.astype(bf16)
        for b in range(2):
            pieces = [
                dot(lifted, up[:, (2 * a + b) * depth : (2 * a + b + 1) * depth]).reshape(
                    HALF, 1, HWIDE, depth
                )
                for a in range(2)
            ]
            both = jnp.concatenate(pieces, axis=1).reshape(cells // 2, depth)
            for h in range(depth // 128):
                stream_halves[h][pl.ds(b, cells // 2, stride=2), :] = both[
                    :, h * 128 : (h + 1) * 128
                ]
        for at in range(0, cells, tile):
            now = stream[at : at + tile, :] + jnp.concatenate(
                [half[at : at + tile, :] for half in stream_halves], axis=1
            )
            stream[at : at + tile, :] = now
            put_act(field_a, WIDE + at, now, WIDE, SIDE)
        for at in range(0, cells, tile):
            now = stream[at : at + tile, :] + conv_rows(
                field_a, level_one.at[2], at, tile, WIDE
            )
            stream[at : at + tile, :] = now
            put_act(field_b, WIDE + at, now, WIDE, SIDE)
        for at in range(0, cells, tile):
            now = stream[at : at + tile, :] + conv_rows(
                field_b, level_one.at[3], at, tile, WIDE
            )
            coarse[at : at + tile, :] = jax.nn.gelu(now).astype(bf16)
        score = lax.dot_general(
            out_t[...], coarse[...], (((1,), (1,)), ((), ())), preferred_element_type=f32
        )
        purified[n] = (
            pixels[n] + step_size * score[0:8, :] + noise_gain * noise[n]
        )
        return carry

    stream_halves = [halves.at[h] for h in range(depth // 128)]
    coarse[cells:, :] = jnp.zeros((coarse.shape[0] - cells, depth), bf16)
    lax.fori_loop(0, pixels.shape[0], one_image, 0)
    for swap in swaps:
        swap.wait()


def run_score(pixels, noise, stem, level_one, down, level_two, up, out_t, mlp_in, mlp_out):
    depth = stem.shape[1]
    vmem = pl.BlockSpec(memory_space=pltpu.VMEM)
    anywhere = pl.BlockSpec(memory_space=pl.ANY)
    return pl.pallas_call(
        score_kernel,
        out_shape=(
            jax.ShapeDtypeStruct(pixels.shape, f32),
            jax.ShapeDtypeStruct((mlp_in.shape[0], mlp_in.shape[1] // 2), bf16),
            jax.ShapeDtypeStruct((mlp_out.shape[0] // 2, mlp_out.shape[1]), bf16),
        ),
        in_specs=[vmem] * 8 + [anywhere] * 2,
        out_specs=(vmem, anywhere, anywhere),
        scratch_shapes=[
            pltpu.VMEM(((SIDE + 2) * WIDE, 3 * depth), bf16),
            pltpu.VMEM(((SIDE + 2) * WIDE, 3 * depth), bf16),
            pltpu.VMEM(((HALF + 2) * HWIDE, 3 * depth), bf16),
            pltpu.VMEM(((HALF + 2) * HWIDE, 3 * depth), bf16),
            pltpu.VMEM((SIDE * WIDE, depth), f32),
            pltpu.VMEM((depth // 128, SIDE * WIDE, 128), f32),
            pltpu.VMEM((WIDE * WIDE, depth), bf16),
            pltpu.SemaphoreType.DMA((2,)),
            pltpu.SemaphoreType.DMA((2,)),
        ],
        compiler_params=pltpu.CompilerParams(
            collective_id=0, has_side_effects=True, vmem_limit_bytes=48 * MIB
        ),
        cost_estimate=pl.CostEstimate(
            flops=10_000_000_000, bytes_accessed=30_000_000, transcendentals=0
        ),
    )(pixels, noise, stem, level_one, down, level_two, up, out_t, mlp_in, mlp_out)


def mlp_kernel(
    rows,
    cols,
    chunk,
    patches,
    embed_weight,
    embed_bias,
    mlp_in,
    in_swapped,
    mlp_out,
    out_swapped,
    encoded,
    own_patches,
    row_patches,
    all_patches,
    embed_w,
    w_in,
    w_out,
    values,
    normed,
    partial_out,
    partial_in,
    hidden,
    total,
    pair_out,
    pair_in,
    last_out,
    last_in,
    load_sem,
    gather_send,
    gather_recv,
    spread_send,
    spread_recv,
    rs_send,
    rs_recv,
    ag_send,
    ag_recv,
    pair_sem,
    last_send,
    last_recv,
):
    row = lax.axis_index("row")
    col = lax.axis_index("col")
    z = col // 2
    core = col % 2
    depth = cols // 2
    last = depth - 1
    sibling = {"col": col + 1 - 2 * core}
    width = w_in.shape[2]
    height = w_out.shape[1]

    loads = [
        pltpu.make_async_copy(embed_weight, embed_w, load_sem.at[0]),
        pltpu.make_async_copy(
            mlp_in.at[:, pl.ds(pl.multiple_of(core * width, 128), width)],
            w_in.at[core],
            load_sem.at[1],
        ),
        pltpu.make_async_copy(in_swapped, w_in.at[1 - core], load_sem.at[2]),
        pltpu.make_async_copy(
            mlp_out.at[pl.ds(pl.multiple_of(core * height, 16), height), :],
            w_out.at[core],
            load_sem.at[3],
        ),
        pltpu.make_async_copy(out_swapped, w_out.at[1 - core], load_sem.at[4]),
    ]
    for load in loads:
        load.start()
    own_patches[...] = patches[...]

    barrier = pltpu.get_barrier_semaphore()
    for step in range(1, cols):
        pl.semaphore_signal(
            barrier, inc=1, device_id={"col": (col + step) % cols}, device_id_type=MESH
        )
    for step in range(1, rows):
        pl.semaphore_signal(
            barrier, inc=1, device_id={"row": (row + step) % rows}, device_id_type=MESH
        )
    pl.semaphore_wait(barrier, cols - 1 + rows - 1)

    gathers = [
        remote(
            own_patches,
            row_patches.at[col],
            gather_send.at[step],
            gather_recv.at[step],
            {"col": (col + step) % cols},
        )
        for step in range(1, cols)
    ]
    for gather in gathers:
        gather.start()
    row_patches[col] = own_patches[...]
    for gather in gathers:
        gather.wait_recv()
    per_row = row_patches.shape[0] * row_patches.shape[1]
    all_patches[row] = row_patches[...].reshape(per_row, row_patches.shape[2]).astype(bf16)
    spreads = [
        remote(
            all_patches.at[row],
            all_patches.at[row],
            spread_send.at[step],
            spread_recv.at[step],
            {"row": (row + step) % rows},
        )
        for step in range(1, rows)
    ]
    for spread in spreads:
        spread.start()
    loads[0].wait()
    for spread in spreads:
        spread.wait_recv()

    tokens = rows * per_row
    pixels = embed_w.shape[0]
    features = embed_w.shape[1]
    span = features // cols

    def embed(at):
        at = pl.multiple_of(at, 128)
        tokens_in = all_patches[...].reshape(tokens, all_patches.shape[2])[:, 0:pixels]
        return (
            (dot(tokens_in, embed_w[:, pl.ds(at, span)]) + embed_bias[0:1, pl.ds(at, span)])
            .astype(bf16)
            .astype(f32)
        )

    def add_statistics(step, sums):
        part = embed(step * span)
        return (
            sums[0] + jnp.sum(part, axis=1, keepdims=True),
            sums[1] + jnp.sum(part * part, axis=1, keepdims=True),
        )

    zeros = jnp.zeros((tokens, 1), f32)
    value_sums, square_sums = lax.fori_loop(0, cols, add_statistics, (zeros, zeros))
    mean = value_sums / features
    scale = lax.rsqrt(square_sums / features - mean * mean + ln_epsilon)
    for j in range(2):
        part = embed((2 * z + j) * span)
        values[j] = part
        normed[j] = ((part - mean) * scale).astype(bf16)
        total[j] = jnp.zeros((tokens, span), f32)
    for load in loads[1:]:
        load.wait()

    chunks = partial_out.shape[1]
    place = (z, last - z)
    ahead = ({"col": col + 2}, {"col": col - 2})
    behind = ({"col": col - 2}, {"col": col + 2})

    def rs_copy(d, i):
        return remote(
            partial_out.at[d, i], partial_in.at[d, i], rs_send.at[d, i], rs_recv.at[d, i], ahead[d]
        )

    def ag_copy(d, i):
        return remote(
            hidden.at[d, i], hidden.at[d, i], ag_send.at[d, i], ag_recv.at[d, i], behind[d]
        )

    def second(d, i):
        at = pl.multiple_of((d * chunks + i) * chunk, chunk)
        for j in range(2):
            total[j] += dot(hidden[d, i], w_out[j, pl.ds(at, chunk), :])

    def slot(t, carry):
        for d in range(2):
            i = t - place[d]

            @pl.when((i >= 0) & (i < chunks))
            def _():
                at = pl.multiple_of((d * chunks + i) * chunk, chunk)
                mine = dot(normed[0], w_in[0, :, pl.ds(at, chunk)]) + dot(
                    normed[1], w_in[1, :, pl.ds(at, chunk)]
                )

                @pl.when(place[d] == 0)
                def _():
                    partial_out[d, i] = mine.astype(bf16)

                @pl.when(place[d] > 0)
                def _():
                    rs_copy(d, i).wait_recv()
                    whole = mine + partial_in[d, i].astype(f32)

                    @pl.when(place[d] < last)
                    def _():
                        partial_out[d, i] = whole.astype(bf16)

                    @pl.when(place[d] == last)
                    def _():
                        hidden[d, i] = jax.nn.gelu(whole).astype(bf16)

                @pl.when(place[d] < last)
                def _():
                    rs_copy(d, i).start()

                @pl.when(place[d] == last)
                def _():
                    ag_copy(d, i).start()
                    second(d, i)

        for d in range(2):
            i = t - (2 * last - place[d])

            @pl.when((i >= 0) & (i < chunks) & (place[d] < last))
            def _():
                ag_copy(d, i).wait_recv()

                @pl.when(place[d] > 0)
                def _():
                    ag_copy(d, i).start()

                second(d, i)

        return carry

    lax.fori_loop(0, chunks + 2 * last, slot, 0)

    pair_out[...] = total[1 - core].astype(bf16)
    pair = remote(pair_out, pair_in, pair_sem.at[0], pair_sem.at[1], sibling)
    pair.start()
    pair.wait_recv()
    summed = total[core] + pair_in[...].astype(f32)
    last_out[...] = summed.astype(bf16).reshape(last_out.shape)
    finals = [
        remote(
            last_out.at[(row + step) % rows],
            last_in.at[step],
            last_send.at[step],
            last_recv.at[step],
            {"row": (row + step) % rows},
        )
        for step in range(1, rows)
    ]
    for final in finals:
        final.start()
    result = values[core, pl.ds(pl.multiple_of(row * per_row, 16), per_row), :]
    result = result + last_out[row].astype(f32)
    for step, final in enumerate(finals):
        final.wait_recv()
        result = result + last_in[step + 1].astype(f32)
    encoded[...] = result.astype(bf16)

    for copy in gathers + spreads + finals + [pair]:
        copy.wait_send()

    def drain(i, carry):
        for d in range(2):

            @pl.when(place[d] < last)
            def _():
                rs_copy(d, i).wait_send()

            @pl.when(place[d] > 0)
            def _():
                ag_copy(d, i).wait_send()

        return carry

    lax.fori_loop(0, chunks, drain, 0)


def run_mlp(
    rows, cols, patches, embed_weight, embed_bias, mlp_in, in_swapped, mlp_out, out_swapped
):
    per_device, pixels = patches.shape
    per_row = cols * per_device
    tokens = rows * per_row
    features = embed_weight.shape[1]
    span = features // cols
    width = in_swapped.shape[1]
    chunk = min(256, width // 2)
    chunks = width // 2 // chunk
    vmem = pl.BlockSpec(memory_space=pltpu.VMEM)
    anywhere = pl.BlockSpec(memory_space=pl.ANY)
    dma = pltpu.SemaphoreType.DMA
    return pl.pallas_call(
        functools.partial(mlp_kernel, rows, cols, chunk),
        out_shape=jax.ShapeDtypeStruct((per_row, span), bf16),
        in_specs=[vmem, anywhere, vmem, anywhere, anywhere, anywhere, anywhere],
        out_specs=vmem,
        scratch_shapes=[
            pltpu.VMEM((per_device, pixels), f32),
            pltpu.VMEM((cols, per_device, pixels), f32),
            pltpu.VMEM((rows, per_row, pixels), bf16),
            pltpu.VMEM(embed_weight.shape, bf16),
            pltpu.VMEM((2,) + in_swapped.shape, bf16),
            pltpu.VMEM((2,) + out_swapped.shape, bf16),
            pltpu.VMEM((2, tokens, span), f32),
            pltpu.VMEM((2, tokens, span), bf16),
            pltpu.VMEM((2, chunks, tokens, chunk), bf16),
            pltpu.VMEM((2, chunks, tokens, chunk), bf16),
            pltpu.VMEM((2, chunks, tokens, chunk), bf16),
            pltpu.VMEM((2, tokens, span), f32),
            pltpu.VMEM((tokens, span), bf16),
            pltpu.VMEM((tokens, span), bf16),
            pltpu.VMEM((rows, per_row, span), bf16),
            pltpu.VMEM((rows, per_row, span), bf16),
            dma((5,)),
            dma((cols,)),
            dma((cols,)),
            dma((rows,)),
            dma((rows,)),
            dma((2, chunks)),
            dma((2, chunks)),
            dma((2, chunks)),
            dma((2, chunks)),
            dma((2,)),
            dma((rows,)),
            dma((rows,)),
        ],
        compiler_params=pltpu.CompilerParams(
            collective_id=1, has_side_effects=True, vmem_limit_bytes=56 * MIB
        ),
        cost_estimate=pl.CostEstimate(
            flops=10_000_000_000, bytes_accessed=30_000_000, transcendentals=0
        ),
    )(patches, embed_weight, embed_bias, mlp_in, in_swapped, mlp_out, out_swapped)


def to_planes(field):
    moved = jnp.pad(
        field.transpose(0, 3, 1, 2), ((0, 0), (0, 5), (0, WIDE - SIDE), (0, WIDE - SIDE))
    )
    return moved.reshape(field.shape[0], 8, WIDE * WIDE)


def on_device(
    images,
    noise_field,
    stem_weight,
    level_one,
    down_weight,
    level_two,
    up_weight,
    out_weight,
    embed_weight,
    embed_bias,
    mlp_in,
    mlp_out,
):
    rows = lax.axis_size("row")
    cols = lax.axis_size("col")
    depth = stem_weight.shape[1]
    stem = jnp.pad(stem_weight.reshape(9, 3, depth), ((0, 7), (0, 5), (0, 0))).reshape(128, depth)
    out_t = jnp.pad(out_weight.T, ((0, 13), (0, 0)))
    planes, in_swapped, out_swapped = run_score(
        to_planes(images),
        to_planes(noise_field),
        stem,
        level_one,
        down_weight,
        level_two,
        up_weight,
        out_t,
        mlp_in,
        mlp_out,
    )
    count = images.shape[0]
    planes = planes.reshape(count, 8, WIDE, WIDE)[:, 0:3, 0:SIDE, 0:SIDE]
    purified = planes.transpose(0, 2, 3, 1)
    grid = SIDE // PATCH
    patches = planes.astype(bf16).reshape(count, 3, grid, PATCH, grid, PATCH)
    patches = patches.transpose(0, 2, 4, 3, 5, 1).reshape(count * grid * grid, PATCH * PATCH * 3)
    pixels = patches.shape[1]
    patches = jnp.pad(patches.astype(f32), ((0, 0), (0, -pixels % 128)))
    encoded = run_mlp(
        rows,
        cols,
        patches,
        embed_weight,
        embed_bias[None, :],
        mlp_in,
        in_swapped,
        mlp_out,
        out_swapped,
    )
    return (purified, encoded)


def solution(mesh):
    placed = (
        P(("row", "col"), None, None, None),
        P(("row", "col"), None, None, None),
        P(),
        P(),
        P(),
        P(),
        P(),
        P(),
        P(),
        P(),
        P("col", "row"),
        P("row", "col"),
    )
    return jax.shard_map(
        on_device,
        mesh=mesh,
        in_specs=placed,
        out_specs=(P(("row", "col"), None, None, None), P("row", "col")),
        check_vma=False,
    )
```

profile of v0, /device:TPU:0, one launch (start us, length us, event | category | flops | bytes accessed | tf_op | source)
XLA Modules:
  0.0 115.1 jit_solution(4545073046192922618)
XLA Ops:
  0.6 0.7 pad.24.out_t
  1.3 0.7 reshape.27
  2.1 0.9 copy.23
  3.0 0.9 copy.24
  3.9 0.1 reshape.26.noise
  4.1 0.1 reshape.25.pixels
  4.2 0.0 copy-start
  4.2 1.7 %copy-done = bf16[2,2304,256]{2,1,0:T(8,128)(2,1)S(1)} copy-done((bf16[2,2304,256]{2,1,0:T(8,128)(2,1)S(1)}, bf16[2,2304,256]{2,1,0:T(8,128)(2,1)}, u32[]{:S(2)}) %copy-start) | copy-done | bytes 2359320
  5.9 0.0 copy-start.1
  5.9 1.0 copy-done.1
  6.9 0.0 copy-start.2
  6.9 1.0 copy-done.2
  7.9 18.5 %shard_map.131 = (f32[2,8,1024]{2,1,0:T(8,128)S(1)}, bf16[768,3072]{1,0:T(8,128)(2,1)}, bf16[3072,768]{1,0:T(8,128)(2,1)}) custom-call(f32[2,8,1024]{2,1,0:T(8,128)S(1)} %reshape.25.pixels, f32[2,8,1024]{2,1,0:T(8,128)S(1)} %reshape.26.noise, bf16[128,256]{1,0:T(8,128)(2,1)S(1)} %pad_bitcast_fusion.stem, bf16[4,2304,256]{2,1,0:T(8,128)(2,1)} %level_one.1, ...), custom_call_target="tpu_custom_call" | custom-call | flops 10000000000 | bytes 30000000 | tf_op jit(solution)/shard_map/pallas_call | solution.py:224
  26.5 0.1 reshape.29
  26.6 0.1 copy.27
  26.7 0.7 copy.28
  27.4 0.1 convert_element_type.23
  27.5 0.8 copy.21
  28.3 0.4 convert_element_type.25
  28.7 0.6 pad_convert_fusion.patches
  29.3 84.3 %shard_map.132 = bf16[64,768]{1,0:T(8,128)(2,1)} custom-call(f32[8,640]{1,0:T(8,128)} %pad_convert_fusion.patches, bf16[588,6144]{1,0:T(8,128)(2,1)} %embed_weight.1, f32[1,6144]{1,0:T(1,128)} %bitcast.21, bf16[768,6144]{1,0:T(8,128)(2,1)} %mlp_in.3, bf16[768,3072]{1,0:T(8,128)(2,1)} %get-tuple-element.6.in_swapped, bf16[6144,768]{1,0:T(8,128)(2,1)} %mlp_out.3, ...), custom_call_target="tpu_custom_call" | custom-call | flops 10000000000 | bytes 30000000 | tf_op jit(solution)/shard_map/pallas_call | solution.py:532
  113.6 1.5 %copy.30 = bf16[64,768]{1,0:T(8,128)(2,1)} copy(bf16[64,768]{1,0:T(8,128)(2,1)} %shard_map.132) | data formatting | bytes 196608
  (4 shorter events, 0.1 us)
Async XLA Ops:
  4.2 1.7 %copy-start = (bf16[2,2304,256]{2,1,0:T(8,128)(2,1)S(1)}, bf16[2,2304,256]{2,1,0:T(8,128)(2,1)}, u32[]{:S(2)}) copy-start(bf16[2,2304,256]{2,1,0:T(8,128)(2,1)} %level_two.1) | copy-start | bytes 7077892
  5.9 1.0 copy-start.1
  6.9 1.0 copy-start.2
where the time goes:
time: 116 us; the launch traced here: 115 us
  Pallas kernels  103 us (89%)
  local copies, waits for them, and re-layouts  11.1 us (10%)
    pallas_call x1, Pallas kernels, run_mlp(): pl.pallas_call(functools.partial(mlp_kernel, rows, cols, chunk), out_shap...  84.3 us
    pallas_call x1, Pallas kernels, run_score(): pl.pallas_call(score_kernel, out_shape=(jax.ShapeDtypeStruct(pixels.shape...  18.5 us
    unnamed x11, local copies, waits for them, and re-layouts  7.85 us

commit v1 on v0

--- a/solution.py
+++ b/solution.py
@@ -17,6 +17,7 @@
 step_size = 0.25
 noise_gain = math.sqrt(0.5)
 ln_epsilon = 1e-06
+LAG = 2
 MESH = pl.DeviceIdType.MESH
 MIB = 1024 * 1024
 f32 = jnp.float32
@@ -68,16 +69,18 @@
     pixels,
     noise,
     stem,
+    level_one_hbm,
+    down_hbm,
+    level_two_hbm,
+    up_hbm,
+    out_t,
+    mlp_in,
+    purified,
+    in_swapped,
     level_one,
     down,
     level_two,
     up,
-    out_t,
-    mlp_in,
-    mlp_out,
-    purified,
-    in_swapped,
-    out_swapped,
     field_a,
     field_b,
     coarse_a,
@@ -85,9 +88,18 @@
     stream,
     halves,
     coarse,
-    send_sem,
-    recv_sem,
+    load_sem,
+    swap_sem,
 ):
+    loads = [
+        pltpu.make_async_copy(level_one_hbm.at[k], level_one.at[k], load_sem.at[k])
+        for k in range(4)
+    ]
+    loads.append(pltpu.make_async_copy(down_hbm, down, load_sem.at[4]))
+    loads.append(pltpu.make_async_copy(level_two_hbm, level_two, load_sem.at[5]))
+    loads.append(pltpu.make_async_copy(up_hbm, up, load_sem.at[6]))
+    for k in (0, 1, 4, 5, 6, 2, 3):
+        loads[k].start()
     col = lax.axis_index("col")
     core = col % 2
     sibling = {"col": col + 1 - 2 * core}
@@ -95,25 +107,14 @@
     pl.semaphore_signal(barrier, inc=1, device_id=sibling, device_id_type=MESH)
     pl.semaphore_wait(barrier, 1)
     width = mlp_in.shape[1] // 2
-    height = mlp_out.shape[0] // 2
-    swaps = [
-        remote(
-            mlp_in.at[:, pl.ds(pl.multiple_of((1 - core) * width, 128), width)],
-            in_swapped,
-            send_sem.at[0],
-            recv_sem.at[0],
-            sibling,
-        ),
-        remote(
-            mlp_out.at[pl.ds(pl.multiple_of((1 - core) * height, 16), height), :],
-            out_swapped,
-            send_sem.at[1],
-            recv_sem.at[1],
-            sibling,
-        ),
-    ]
-    for swap in swaps:
-        swap.start()
+    swap = remote(
+        mlp_in.at[:, pl.ds(pl.multiple_of((1 - core) * width, 128), width)],
+        in_swapped,
+        swap_sem.at[0],
+        swap_sem.at[1],
+        sibling,
+    )
+    swap.start()
 
     depth = stream.shape[1]
     cells = SIDE * WIDE
@@ -129,6 +130,12 @@
         field[row + last : row + last + row, :] = jnp.zeros((row, 3 * depth), bf16)
 
     def one_image(n, carry):
+        def arrived(*which):
+            @pl.when(n == 0)
+            def _():
+                for k in which:
+                    loads[k].wait()
+
         view = pixels[n].astype(bf16).astype(f32)
         lanes = view.shape[1]
         groups = []
@@ -142,12 +149,14 @@
             now = dot(columns[at : at + tile, :], stem[...])
             stream[at : at + tile, :] = now
             put_act(field_a, WIDE + at, now, WIDE, SIDE)
+        arrived(0)
         for at in range(0, cells, tile):
             now = stream[at : at + tile, :] + conv_rows(
                 field_a, level_one.at[0], at, tile, WIDE
             )
             stream[at : at + tile, :] = now
             put_act(field_b, WIDE + at, now, WIDE, SIDE)
+        arrived(1)
         for at in range(0, cells, tile):
             now = stream[at : at + tile, :] + conv_rows(
                 field_b, level_one.at[1], at, tile, WIDE
@@ -155,6 +164,7 @@
             stream[at : at + tile, :] = now
             for h in range(depth // 128):
                 stream_halves[h][at : at + tile, :] = now[:, h * 128 : (h + 1) * 128]
+        arrived(4, 5, 6)
         now = None
         for b in range(2):
             parts = [
@@ -191,6 +201,7 @@
             )
             stream[at : at + tile, :] = now
             put_act(field_a, WIDE + at, now, WIDE, SIDE)
+        arrived(2, 3)
         for at in range(0, cells, tile):
             now = stream[at : at + tile, :] + conv_rows(
                 field_a, level_one.at[2], at, tile, WIDE
@@ -213,11 +224,10 @@
     stream_halves = [halves.at[h] for h in range(depth // 128)]
     coarse[cells:, :] = jnp.zeros((coarse.shape[0] - cells, depth), bf16)
     lax.fori_loop(0, pixels.shape[0], one_image, 0)
-    for swap in swaps:
-        swap.wait()
-
-
-def run_score(pixels, noise, stem, level_one, down, level_two, up, out_t, mlp_in, mlp_out):
+    swap.wait()
+
+
+def run_score(pixels, noise, stem, level_one, down, level_two, up, out_t, mlp_in):
     depth = stem.shape[1]
     vmem = pl.BlockSpec(memory_space=pltpu.VMEM)
     anywhere = pl.BlockSpec(memory_space=pl.ANY)
@@ -226,11 +236,14 @@
         out_shape=(
             jax.ShapeDtypeStruct(pixels.shape, f32),
             jax.ShapeDtypeStruct((mlp_in.shape[0], mlp_in.shape[1] // 2), bf16),
-            jax.ShapeDtypeStruct((mlp_out.shape[0] // 2, mlp_out.shape[1]), bf16),
         ),
-        in_specs=[vmem] * 8 + [anywhere] * 2,
-        out_specs=(vmem, anywhere, anywhere),
+        in_specs=[vmem] * 3 + [anywhere] * 4 + [vmem, anywhere],
+        out_specs=(vmem, anywhere),
         scratch_shapes=[
+            pltpu.VMEM(level_one.shape, bf16),
+            pltpu.VMEM(down.shape, bf16),
+            pltpu.VMEM(level_two.shape, bf16),
+            pltpu.VMEM(up.shape, bf16),
             pltpu.VMEM(((SIDE + 2) * WIDE, 3 * depth), bf16),
             pltpu.VMEM(((SIDE + 2) * WIDE, 3 * depth), bf16),
             pltpu.VMEM(((HALF + 2) * HWIDE, 3 * depth), bf16),
@@ -238,16 +251,16 @@
             pltpu.VMEM((SIDE * WIDE, depth), f32),
             pltpu.VMEM((depth // 128, SIDE * WIDE, 128), f32),
             pltpu.VMEM((WIDE * WIDE, depth), bf16),
-            pltpu.SemaphoreType.DMA((2,)),
+            pltpu.SemaphoreType.DMA((7,)),
             pltpu.SemaphoreType.DMA((2,)),
         ],
         compiler_params=pltpu.CompilerParams(
-            collective_id=0, has_side_effects=True, vmem_limit_bytes=48 * MIB
+            collective_id=0, has_side_effects=True, vmem_limit_bytes=60 * MIB
         ),
         cost_estimate=pl.CostEstimate(
             flops=10_000_000_000, bytes_accessed=30_000_000, transcendentals=0
         ),
-    )(pixels, noise, stem, level_one, down, level_two, up, out_t, mlp_in, mlp_out)
+    )(pixels, noise, stem, level_one, down, level_two, up, out_t, mlp_in)
 
 
 def mlp_kernel(
@@ -260,7 +273,6 @@
     mlp_in,
     in_swapped,
     mlp_out,
-    out_swapped,
     encoded,
     own_patches,
     row_patches,
@@ -268,8 +280,10 @@
     embed_w,
     w_in,
     w_out,
+    w_other,
     values,
     normed,
+    mine,
     partial_out,
     partial_in,
     hidden,
@@ -287,7 +301,9 @@
     rs_recv,
     ag_send,
     ag_recv,
-    pair_sem,
+    swap_sem,
+    pair_send,
+    pair_recv,
     last_send,
     last_recv,
 ):
@@ -299,7 +315,7 @@
     last = depth - 1
     sibling = {"col": col + 1 - 2 * core}
     width = w_in.shape[2]
-    height = w_out.shape[1]
+    height = w_out.shape[0]
 
     loads = [
         pltpu.make_async_copy(embed_weight, embed_w, load_sem.at[0]),
@@ -311,10 +327,9 @@
         pltpu.make_async_copy(in_swapped, w_in.at[1 - core], load_sem.at[2]),
         pltpu.make_async_copy(
             mlp_out.at[pl.ds(pl.multiple_of(core * height, 16), height), :],
-            w_out.at[core],
+            w_out,
             load_sem.at[3],
         ),
-        pltpu.make_async_copy(out_swapped, w_out.at[1 - core], load_sem.at[4]),
     ]
     for load in loads:
         load.start()
@@ -363,6 +378,14 @@
     loads[0].wait()
     for spread in spreads:
         spread.wait_recv()
+    swap = remote(
+        mlp_out.at[pl.ds(pl.multiple_of((1 - core) * height, 16), height), :],
+        w_other,
+        swap_sem.at[0],
+        swap_sem.at[1],
+        sibling,
+    )
+    swap.start()
 
     tokens = rows * per_row
     pixels = embed_w.shape[0]
@@ -394,8 +417,8 @@
         values[j] = part
         normed[j] = ((part - mean) * scale).astype(bf16)
         total[j] = jnp.zeros((tokens, span), f32)
-    for load in loads[1:]:
-        load.wait()
+    loads[1].wait()
+    loads[2].wait()
 
     chunks = partial_out.shape[1]
     place = (z, last - z)
@@ -412,30 +435,45 @@
             hidden.at[d, i], hidden.at[d, i], ag_send.at[d, i], ag_recv.at[d, i], behind[d]
         )
 
-    def second(d, i):
-        at = pl.multiple_of((d * chunks + i) * chunk, chunk)
-        for j in range(2):
-            total[j] += dot(hidden[d, i], w_out[j, pl.ds(at, chunk), :])
-
     def slot(t, carry):
+        @pl.when(t == LAG * last)
+        def _():
+            loads[3].wait()
+            swap.wait_recv()
+
         for d in range(2):
-            i = t - place[d]
+            i = t - LAG * (2 * last - place[d])
+
+            @pl.when((i >= 0) & (i < chunks) & (place[d] < last))
+            def _():
+                ag_copy(d, i).wait_recv()
+
+                @pl.when(place[d] > 0)
+                def _():
+                    ag_copy(d, i).start()
+
+        for d in range(2):
+            i = t - LAG * place[d]
 
             @pl.when((i >= 0) & (i < chunks))
             def _():
-                at = pl.multiple_of((d * chunks + i) * chunk, chunk)
-                mine = dot(normed[0], w_in[0, :, pl.ds(at, chunk)]) + dot(
-                    normed[1], w_in[1, :, pl.ds(at, chunk)]
-                )
+                @pl.when(i % 2 == 0)
+                def _():
+                    at = pl.multiple_of((d * chunks + i) * chunk, 2 * chunk)
+                    both = dot(normed[0], w_in[0, :, pl.ds(at, 2 * chunk)]) + dot(
+                        normed[1], w_in[1, :, pl.ds(at, 2 * chunk)]
+                    )
+                    mine[d, 0] = both[:, 0:chunk]
+                    mine[d, 1] = both[:, chunk : 2 * chunk]
 
                 @pl.when(place[d] == 0)
                 def _():
-                    partial_out[d, i] = mine.astype(bf16)
+                    partial_out[d, i] = mine[d, i % 2].astype(bf16)
 
                 @pl.when(place[d] > 0)
                 def _():
                     rs_copy(d, i).wait_recv()
-                    whole = mine + partial_in[d, i].astype(f32)
+                    whole = mine[d, i % 2] + partial_in[d, i].astype(f32)
 
                     @pl.when(place[d] < last)
                     def _():
@@ -452,51 +490,55 @@
                 @pl.when(place[d] == last)
                 def _():
                     ag_copy(d, i).start()
-                    second(d, i)
 
         for d in range(2):
-            i = t - (2 * last - place[d])
-
-            @pl.when((i >= 0) & (i < chunks) & (place[d] < last))
+            i = t - LAG * (2 * last - place[d])
+
+            @pl.when((i >= 0) & (i < chunks) & (i % 2 == 1))
             def _():
-                ag_copy(d, i).wait_recv()
-
-                @pl.when(place[d] > 0)
-                def _():
-                    ag_copy(d, i).start()
-
-                second(d, i)
+                at = pl.multiple_of((d * chunks + i - 1) * chunk, 2 * chunk)
+                units = jnp.concatenate([hidden[d, i - 1], hidden[d, i]], axis=1)
+                total[0] += dot(units, w_out[pl.ds(at, 2 * chunk), :])
+                total[1] += dot(units, w_other[pl.ds(at, 2 * chunk), :])
 
         return carry
 
-    lax.fori_loop(0, chunks + 2 * last, slot, 0)
-
-    pair_out[...] = total[1 - core].astype(bf16)
-    pair = remote(pair_out, pair_in, pair_sem.at[0], pair_sem.at[1], sibling)
-    pair.start()
-    pair.wait_recv()
-    summed = total[core] + pair_in[...].astype(f32)
-    last_out[...] = summed.astype(bf16).reshape(last_out.shape)
-    finals = [
-        remote(
-            last_out.at[(row + step) % rows],
-            last_in.at[step],
-            last_send.at[step],
-            last_recv.at[step],
-            {"row": (row + step) % rows},
-        )
-        for step in range(1, rows)
-    ]
-    for final in finals:
-        final.start()
-    result = values[core, pl.ds(pl.multiple_of(row * per_row, 16), per_row), :]
-    result = result + last_out[row].astype(f32)
+    lax.fori_loop(0, chunks + 2 * LAG * last, slot, 0)
+
+    pairs, finals = [], []
+    for step in list(range(1, rows)) + [0]:
+        block = (row + step) % rows
+        at = pl.ds(pl.multiple_of(block * per_row, 16), per_row)
+        pair_out[step] = total[1, at, :].astype(bf16)
+        pair = remote(
+            pair_out.at[step], pair_in.at[step], pair_send.at[step], pair_recv.at[step], sibling
+        )
+        pair.start()
+        pairs.append(pair)
+    for step in list(range(1, rows)) + [0]:
+        block = (row + step) % rows
+        at = pl.ds(pl.multiple_of(block * per_row, 16), per_row)
+        pairs[step - 1].wait_recv()
+        summed = total[0, at, :] + pair_in[step].astype(f32)
+        if step == 0:
+            result = values[core, at, :] + summed
+        else:
+            last_out[step] = summed.astype(bf16)
+            final = remote(
+                last_out.at[step],
+                last_in.at[step],
+                last_send.at[step],
+                last_recv.at[step],
+                {"row": block},
+            )
+            final.start()
+            finals.append(final)
     for step, final in enumerate(finals):
         final.wait_recv()
         result = result + last_in[step + 1].astype(f32)
     encoded[...] = result.astype(bf16)
 
-    for copy in gathers + spreads + finals + [pair]:
+    for copy in gathers + spreads + finals + pairs + [swap]:
         copy.wait_send()
 
     def drain(i, carry):
@@ -516,7 +558,7 @@
 
 
 def run_mlp(
-    rows, cols, patches, embed_weight, embed_bias, mlp_in, in_swapped, mlp_out, out_swapped
+    rows, cols, patches, embed_weight, embed_bias, mlp_in, in_swapped, mlp_out
 ):
     per_device, pixels = patches.shape
     per_row = cols * per_device
@@ -524,7 +566,7 @@
     features = embed_weight.shape[1]
     span = features // cols
     width = in_swapped.shape[1]
-    chunk = min(256, width // 2)
+    chunk = min(128, width // 2)
     chunks = width // 2 // chunk
     vmem = pl.BlockSpec(memory_space=pltpu.VMEM)
     anywhere = pl.BlockSpec(memory_space=pl.ANY)
@@ -532,7 +574,7 @@
     return pl.pallas_call(
         functools.partial(mlp_kernel, rows, cols, chunk),
         out_shape=jax.ShapeDtypeStruct((per_row, span), bf16),
-        in_specs=[vmem, anywhere, vmem, anywhere, anywhere, anywhere, anywhere],
+        in_specs=[vmem, anywhere, vmem, anywhere, anywhere, anywhere],
         out_specs=vmem,
         scratch_shapes=[
             pltpu.VMEM((per_device, pixels), f32),
@@ -540,18 +582,20 @@
             pltpu.VMEM((rows, per_row, pixels), bf16),
             pltpu.VMEM(embed_weight.shape, bf16),
             pltpu.VMEM((2,) + in_swapped.shape, bf16),
-            pltpu.VMEM((2,) + out_swapped.shape, bf16),
+            pltpu.VMEM((width, span), bf16),
+            pltpu.VMEM((width, span), bf16),
             pltpu.VMEM((2, tokens, span), f32),
             pltpu.VMEM((2, tokens, span), bf16),
+            pltpu.VMEM((2, 2, tokens, chunk), f32),
             pltpu.VMEM((2, chunks, tokens, chunk), bf16),
             pltpu.VMEM((2, chunks, tokens, chunk), bf16),
             pltpu.VMEM((2, chunks, tokens, chunk), bf16),
             pltpu.VMEM((2, tokens, span), f32),
-            pltpu.VMEM((tokens, span), bf16),
-            pltpu.VMEM((tokens, span), bf16),
             pltpu.VMEM((rows, per_row, span), bf16),
             pltpu.VMEM((rows, per_row, span), bf16),
-            dma((5,)),
+            pltpu.VMEM((rows, per_row, span), bf16),
+            pltpu.VMEM((rows, per_row, span), bf16),
+            dma((4,)),
             dma((cols,)),
             dma((cols,)),
             dma((rows,)),
@@ -563,6 +607,8 @@
             dma((2,)),
             dma((rows,)),
             dma((rows,)),
+            dma((rows,)),
+            dma((rows,)),
         ],
         compiler_params=pltpu.CompilerParams(
             collective_id=1, has_side_effects=True, vmem_limit_bytes=56 * MIB
@@ -570,7 +616,7 @@
         cost_estimate=pl.CostEstimate(
             flops=10_000_000_000, bytes_accessed=30_000_000, transcendentals=0
         ),
-    )(patches, embed_weight, embed_bias, mlp_in, in_swapped, mlp_out, out_swapped)
+    )(patches, embed_weight, embed_bias, mlp_in, in_swapped, mlp_out)
 
 
 def to_planes(field):
@@ -599,7 +645,7 @@
     depth = stem_weight.shape[1]
     stem = jnp.pad(stem_weight.reshape(9, 3, depth), ((0, 7), (0, 5), (0, 0))).reshape(128, depth)
     out_t = jnp.pad(out_weight.T, ((0, 13), (0, 0)))
-    planes, in_swapped, out_swapped = run_score(
+    planes, in_swapped = run_score(
         to_planes(images),
         to_planes(noise_field),
         stem,
@@ -609,7 +655,6 @@
         up_weight,
         out_t,
         mlp_in,
-        mlp_out,
     )
     count = images.shape[0]
     planes = planes.reshape(count, 8, WIDE, WIDE)[:, 0:3, 0:SIDE, 0:SIDE]
@@ -628,7 +673,6 @@
         mlp_in,
         in_swapped,
         mlp_out,
-        out_swapped,
     )
     return (purified, encoded)
 

time: 116 us -> 114 us (0.983)
  Pallas kernels: 103 us -> 101 us
    unnamed x11 -> x5, local copies, waits for them, and re-layouts: 7.85 us -> 4.11 us
    pallas_call x1, Pallas kernels: 84.3 us -> 81.3 us  [run_mlp(): pl.pallas_call(functools.partial(mlp_kernel, rows, cols, chunk), out_shap...]
    pallas_call x1, Pallas kernels: 18.5 us -> 20.1 us  [run_score(): pl.pallas_call(score_kernel, out_shape=(jax.ShapeDtypeStruct(pixels.shape...]
    reshape x2, local copies, waits for them, and re-layouts: 0.28 us -> 1.54 us  [to_planes(): return moved.reshape(field.shape[0], 8, WIDE * WIDE)]
where the time goes in v1:
time: 114 us; the launch traced here: 113 us
  Pallas kernels  101 us (89%)
  local copies, waits for them, and re-layouts  10.6 us (9%)
    pallas_call x1, Pallas kernels, run_mlp(): pl.pallas_call(functools.partial(mlp_kernel, rows, cols, chunk), out_shap...  81.3 us
    pallas_call x1, Pallas kernels, run_score(): pl.pallas_call(score_kernel, out_shape=(jax.ShapeDtypeStruct(pixels.shape...  20.1 us
    unnamed x5, local copies, waits for them, and re-layouts  4.11 us

profile of v1, /device:TPU:0, one launch (start us, length us, event | category | flops | bytes accessed | tf_op | source)
XLA Modules:
  0.0 113.4 jit_solution(12750414857290971985)
XLA Ops:
  0.6 1.3 %pad.24.out_t = bf16[16,256]{1,0:T(8,128)(2,1)} pad(bf16[3,256]{1,0:T(4,128)(2,1)} %bitcast.20, bf16[]{:T(256)} %constant.5.clone.1), padding=0_13x0_0 | pad | bytes 9730 | tf_op jit(solution)/shard_map/jit(_pad)/pad | solution.py:647
  1.9 0.7 reshape.27
  2.6 0.6 pad_bitcast_fusion.stem
  3.3 0.9 copy.23
  4.2 0.9 copy.24
  5.1 0.8 reshape.26.noise
  5.9 0.8 reshape.25.pixels
  6.7 20.1 %shard_map.131 = (f32[2,8,1024]{2,1,0:T(8,128)}, bf16[768,3072]{1,0:T(8,128)(2,1)}) custom-call(f32[2,8,1024]{2,1,0:T(8,128)} %reshape.25.pixels, f32[2,8,1024]{2,1,0:T(8,128)} %reshape.26.noise, bf16[128,256]{1,0:T(8,128)(2,1)} %pad_bitcast_fusion.stem, bf16[4,2304,256]{2,1,0:T(8,128)(2,1)} %level_one_hbm.1, bf16[1024,256]{1,0:T(8,128)(2,1)} %down_hbm.1, ...), custom_call_target="tpu_custom_call" | custom-call | flops 10000000000 | bytes 30000000 | tf_op jit(solution)/shard_map/pallas_call | solution.py:234
  26.8 1.0 reshape.29
  27.8 0.1 copy.27
  27.9 0.7 copy.28
  28.6 0.1 convert_element_type.23
  28.7 0.8 copy.21
  29.5 0.4 convert_element_type.25
  29.9 0.6 pad_convert_fusion.patches
  30.5 81.3 %shard_map.132 = bf16[64,768]{1,0:T(8,128)(2,1)} custom-call(f32[8,640]{1,0:T(8,128)} %pad_convert_fusion.patches, bf16[588,6144]{1,0:T(8,128)(2,1)} %embed_weight.1, f32[1,6144]{1,0:T(1,128)} %bitcast.21, bf16[768,6144]{1,0:T(8,128)(2,1)} %mlp_in.3, bf16[768,3072]{1,0:T(8,128)(2,1)} %get-tuple-element.5.in_swapped, bf16[6144,768]{1,0:T(8,128)(2,1)} %mlp_out.1), custom_call_target="tpu_custom_call" | custom-call | flops 10000000000 | bytes 30000000 | tf_op jit(solution)/shard_map/pallas_call | solution.py:574
  111.9 1.5 %copy.30 = bf16[64,768]{1,0:T(8,128)(2,1)} copy(bf16[64,768]{1,0:T(8,128)(2,1)} %shard_map.132) | data formatting | bytes 196608
  (3 shorter events, 0.0 us)

commit v2 on v1

--- a/solution.py
+++ b/solution.py
@@ -66,9 +66,9 @@
 
 
 def score_kernel(
-    pixels,
-    noise,
-    stem,
+    images,
+    noise_field,
+    stem_weight,
     level_one_hbm,
     down_hbm,
     level_two_hbm,
@@ -77,6 +77,10 @@
     mlp_in,
     purified,
     in_swapped,
+    pixels,
+    noise,
+    result,
+    stem,
     level_one,
     down,
     level_two,
@@ -117,6 +121,16 @@
     swap.start()
 
     depth = stream.shape[1]
+    count = pixels.shape[0]
+    for planes, given in ((pixels, images), (noise, noise_field)):
+        planes[...] = jnp.zeros(planes.shape, f32)
+        for n in range(count):
+            for y in range(SIDE):
+                planes[n, 0:3, y * WIDE : y * WIDE + SIDE] = given[y, :, n, :]
+    stem[...] = jnp.zeros(stem.shape, f32)
+    stem_rows = stem_weight[...].astype(f32)
+    for g in range(9):
+        stem[8 * g : 8 * g + 3, :] = stem_rows[3 * g : 3 * g + 3, :]
     cells = SIDE * WIDE
     ccells = HALF * HWIDE
     tile = 7 * WIDE
@@ -146,7 +160,7 @@
         groups.extend([jnp.zeros_like(view)] * 7)
         columns = jnp.concatenate(groups, axis=0).T.astype(bf16)
         for at in range(0, cells, tile):
-            now = dot(columns[at : at + tile, :], stem[...])
+            now = dot(columns[at : at + tile, :], stem[...].astype(bf16))
             stream[at : at + tile, :] = now
             put_act(field_a, WIDE + at, now, WIDE, SIDE)
         arrived(0)
@@ -216,30 +230,37 @@
         score = lax.dot_general(
             out_t[...], coarse[...], (((1,), (1,)), ((), ())), preferred_element_type=f32
         )
-        purified[n] = (
-            pixels[n] + step_size * score[0:8, :] + noise_gain * noise[n]
+        result[n, 0:3, :] = (
+            pixels[n, 0:3, :] + step_size * score + noise_gain * noise[n, 0:3, :]
         )
         return carry
 
     stream_halves = [halves.at[h] for h in range(depth // 128)]
     coarse[cells:, :] = jnp.zeros((coarse.shape[0] - cells, depth), bf16)
-    lax.fori_loop(0, pixels.shape[0], one_image, 0)
+    lax.fori_loop(0, count, one_image, 0)
+    for n in range(count):
+        for y in range(SIDE):
+            purified[y, :, n, :] = result[n, 0:3, y * WIDE : y * WIDE + SIDE]
     swap.wait()
 
 
-def run_score(pixels, noise, stem, level_one, down, level_two, up, out_t, mlp_in):
+def run_score(images, noise_field, stem, level_one, down, level_two, up, out_t, mlp_in):
     depth = stem.shape[1]
     vmem = pl.BlockSpec(memory_space=pltpu.VMEM)
     anywhere = pl.BlockSpec(memory_space=pl.ANY)
     return pl.pallas_call(
         score_kernel,
         out_shape=(
-            jax.ShapeDtypeStruct(pixels.shape, f32),
+            jax.ShapeDtypeStruct(images.shape, f32),
             jax.ShapeDtypeStruct((mlp_in.shape[0], mlp_in.shape[1] // 2), bf16),
         ),
         in_specs=[vmem] * 3 + [anywhere] * 4 + [vmem, anywhere],
         out_specs=(vmem, anywhere),
         scratch_shapes=[
+            pltpu.VMEM((images.shape[2], 8, WIDE * WIDE), f32),
+            pltpu.VMEM((images.shape[2], 8, WIDE * WIDE), f32),
+            pltpu.VMEM((images.shape[2], 8, WIDE * WIDE), f32),
+            pltpu.VMEM((128, depth), f32),
             pltpu.VMEM(level_one.shape, bf16),
             pltpu.VMEM(down.shape, bf16),
             pltpu.VMEM(level_two.shape, bf16),
@@ -260,7 +281,7 @@
         cost_estimate=pl.CostEstimate(
             flops=10_000_000_000, bytes_accessed=30_000_000, transcendentals=0
         ),
-    )(pixels, noise, stem, level_one, down, level_two, up, out_t, mlp_in)
+    )(images, noise_field, stem, level_one, down, level_two, up, out_t, mlp_in)
 
 
 def mlp_kernel(
@@ -281,9 +302,9 @@
     w_in,
     w_out,
     w_other,
+    statistics,
     values,
     normed,
-    mine,
     partial_out,
     partial_in,
     hidden,
@@ -297,6 +318,8 @@
     gather_recv,
     spread_send,
     spread_recv,
+    share_send,
+    share_recv,
     rs_send,
     rs_recv,
     ag_send,
@@ -375,7 +398,48 @@
     ]
     for spread in spreads:
         spread.start()
+    tokens = rows * per_row
+    part_rows = per_row // 2
+    pixels = embed_w.shape[0]
+    features = embed_w.shape[1]
+    span = features // cols
     loads[0].wait()
+
+    def embed(tokens_in, at):
+        at = pl.multiple_of(at, 128)
+        return (
+            (dot(tokens_in, embed_w[:, pl.ds(at, span)]) + embed_bias[0:1, pl.ds(at, span)])
+            .astype(bf16)
+            .astype(f32)
+        )
+
+    row_tokens = all_patches[row][:, 0:pixels]
+
+    def add_statistics(step, sums):
+        part = embed(row_tokens, step * span)
+        return (
+            sums[0] + jnp.sum(part, axis=1, keepdims=True),
+            sums[1] + jnp.sum(part * part, axis=1, keepdims=True),
+        )
+
+    zeros = jnp.zeros((per_row, 1), f32)
+    value_sums, square_sums = lax.fori_loop(0, cols, add_statistics, (zeros, zeros))
+    mean = value_sums / features
+    scale = lax.rsqrt(square_sums / features - mean * mean + ln_epsilon)
+    lane = lax.broadcasted_iota(jnp.int32, (per_row, 128), 1)
+    statistics[row] = jnp.where(lane < 64, mean, scale)
+    shares = [
+        remote(
+            statistics.at[row],
+            statistics.at[row],
+            share_send.at[step],
+            share_recv.at[step],
+            {"row": (row + step) % rows},
+        )
+        for step in range(1, rows)
+    ]
+    for share in shares:
+        share.start()
     for spread in spreads:
         spread.wait_recv()
     swap = remote(
@@ -387,40 +451,25 @@
     )
     swap.start()
 
-    tokens = rows * per_row
-    pixels = embed_w.shape[0]
-    features = embed_w.shape[1]
-    span = features // cols
-
-    def embed(at):
-        at = pl.multiple_of(at, 128)
-        tokens_in = all_patches[...].reshape(tokens, all_patches.shape[2])[:, 0:pixels]
-        return (
-            (dot(tokens_in, embed_w[:, pl.ds(at, span)]) + embed_bias[0:1, pl.ds(at, span)])
-            .astype(bf16)
-            .astype(f32)
-        )
-
-    def add_statistics(step, sums):
-        part = embed(step * span)
-        return (
-            sums[0] + jnp.sum(part, axis=1, keepdims=True),
-            sums[1] + jnp.sum(part * part, axis=1, keepdims=True),
-        )
-
-    zeros = jnp.zeros((tokens, 1), f32)
-    value_sums, square_sums = lax.fori_loop(0, cols, add_statistics, (zeros, zeros))
-    mean = value_sums / features
-    scale = lax.rsqrt(square_sums / features - mean * mean + ln_epsilon)
+    all_tokens = all_patches[...].reshape(tokens, all_patches.shape[2])[:, 0:pixels]
     for j in range(2):
-        part = embed((2 * z + j) * span)
-        values[j] = part
-        normed[j] = ((part - mean) * scale).astype(bf16)
-        total[j] = jnp.zeros((tokens, span), f32)
+        values[j] = embed(all_tokens, (2 * z + j) * span)
+    for share in shares:
+        share.wait_recv()
+    for half in range(2):
+        rows_in = pl.ds(half * part_rows, part_rows)
+        known = statistics[:, rows_in, :].reshape(tokens // 2, 128)
+        for j in range(2):
+            part = values[j].reshape(rows, per_row, span)[
+                :, half * part_rows : (half + 1) * part_rows
+            ].reshape(tokens // 2, span)
+            normed[j, half] = ((part - known[:, 0:1]) * known[:, 64:65]).astype(bf16)
+            total[j, half] = jnp.zeros((tokens // 2, span), f32)
     loads[1].wait()
     loads[2].wait()
 
     chunks = partial_out.shape[1]
+    per_half = chunks // 2
     place = (z, last - z)
     ahead = ({"col": col + 2}, {"col": col - 2})
     behind = ({"col": col - 2}, {"col": col + 2})
@@ -434,6 +483,48 @@
         return remote(
             hidden.at[d, i], hidden.at[d, i], ag_send.at[d, i], ag_recv.at[d, i], behind[d]
         )
+
+    def pair_copy(half):
+        return remote(
+            pair_out.at[half],
+            pair_in.at[half],
+            pair_send.at[half],
+            pair_recv.at[half],
+            sibling,
+        )
+
+    def final_copies(half):
+        return [
+            remote(
+                last_out.at[half, (row + step) % rows],
+                last_in.at[half, step],
+                last_send.at[half, step],
+                last_recv.at[half, step],
+                {"row": (row + step) % rows},
+            )
+            for step in range(1, rows)
+        ]
+
+    def pair_up(half):
+        pair_out[half] = total[1, half].astype(bf16)
+        pair_copy(half).start()
+
+    def send_final(half):
+        pair_copy(half).wait_recv()
+        summed = total[0, half] + pair_in[half].astype(f32)
+        last_out[half] = summed.astype(bf16).reshape(rows, part_rows, span)
+        for final in final_copies(half):
+            final.start()
+
+    def finish(half):
+        at = pl.ds(pl.multiple_of(row * per_row + half * part_rows, 16), part_rows)
+        result = values[core, at, :] + last_out[half, row].astype(f32)
+        for step, final in enumerate(final_copies(half)):
+            final.wait_recv()
+            result = result + last_in[half, step + 1].astype(f32)
+        encoded[half * part_rows : (half + 1) * part_rows, :] = result.astype(bf16)
+
+    first_done = per_half - 1 + LAG * (2 * last - jnp.minimum(place[0], place[1]))
 
     def slot(t, carry):
         @pl.when(t == LAG * last)
@@ -457,23 +548,20 @@
 
             @pl.when((i >= 0) & (i < chunks))
             def _():
-                @pl.when(i % 2 == 0)
-                def _():
-                    at = pl.multiple_of((d * chunks + i) * chunk, 2 * chunk)
-                    both = dot(normed[0], w_in[0, :, pl.ds(at, 2 * chunk)]) + dot(
-                        normed[1], w_in[1, :, pl.ds(at, 2 * chunk)]
-                    )
-                    mine[d, 0] = both[:, 0:chunk]
-                    mine[d, 1] = both[:, chunk : 2 * chunk]
+                half = i // per_half
+                at = pl.multiple_of((d * per_half + i % per_half) * chunk, chunk)
+                mine = dot(normed[0, half], w_in[0, :, pl.ds(at, chunk)]) + dot(
+                    normed[1, half], w_in[1, :, pl.ds(at, chunk)]
+                )
 
                 @pl.when(place[d] == 0)
                 def _():
-                    partial_out[d, i] = mine[d, i % 2].astype(bf16)
+                    partial_out[d, i] = mine.astype(bf16)
 
                 @pl.when(place[d] > 0)
                 def _():
                     rs_copy(d, i).wait_recv()
-                    whole = mine[d, i % 2] + partial_in[d, i].astype(f32)
+                    whole = mine + partial_in[d, i].astype(f32)
 
                     @pl.when(place[d] < last)
                     def _():
@@ -494,51 +582,33 @@
         for d in range(2):
             i = t - LAG * (2 * last - place[d])
 
-            @pl.when((i >= 0) & (i < chunks) & (i % 2 == 1))
+            @pl.when((i >= 0) & (i < chunks))
             def _():
-                at = pl.multiple_of((d * chunks + i - 1) * chunk, 2 * chunk)
-                units = jnp.concatenate([hidden[d, i - 1], hidden[d, i]], axis=1)
-                total[0] += dot(units, w_out[pl.ds(at, 2 * chunk), :])
-                total[1] += dot(units, w_other[pl.ds(at, 2 * chunk), :])
+                half = i // per_half
+                at = pl.multiple_of((d * per_half + i % per_half) * chunk, chunk)
+                total[0, half] += dot(hidden[d, i], w_out[pl.ds(at, chunk), :])
+                total[1, half] += dot(hidden[d, i], w_other[pl.ds(at, chunk), :])
+
+        @pl.when(t == first_done)
+        def _():
+            pair_up(0)
+
+        @pl.when(t == first_done + 2)
+        def _():
+            send_final(0)
 
         return carry
 
     lax.fori_loop(0, chunks + 2 * LAG * last, slot, 0)
 
-    pairs, finals = [], []
-    for step in list(range(1, rows)) + [0]:
-        block = (row + step) % rows
-        at = pl.ds(pl.multiple_of(block * per_row, 16), per_row)
-        pair_out[step] = total[1, at, :].astype(bf16)
-        pair = remote(
-            pair_out.at[step], pair_in.at[step], pair_send.at[step], pair_recv.at[step], sibling
-        )
-        pair.start()
-        pairs.append(pair)
-    for step in list(range(1, rows)) + [0]:
-        block = (row + step) % rows
-        at = pl.ds(pl.multiple_of(block * per_row, 16), per_row)
-        pairs[step - 1].wait_recv()
-        summed = total[0, at, :] + pair_in[step].astype(f32)
-        if step == 0:
-            result = values[core, at, :] + summed
-        else:
-            last_out[step] = summed.astype(bf16)
-            final = remote(
-                last_out.at[step],
-                last_in.at[step],
-                last_send.at[step],
-                last_recv.at[step],
-                {"row": block},
-            )
-            final.start()
-            finals.append(final)
-    for step, final in enumerate(finals):
-        final.wait_recv()
-        result = result + last_in[step + 1].astype(f32)
-    encoded[...] = result.astype(bf16)
-
-    for copy in gathers + spreads + finals + pairs + [swap]:
+    pair_up(1)
+    finish(0)
+    send_final(1)
+    finish(1)
+
+    finals = [final for half in range(2) for final in final_copies(half)]
+    pairs = [pair_copy(half) for half in range(2)]
+    for copy in gathers + spreads + shares + finals + pairs + [swap]:
         copy.wait_send()
 
     def drain(i, carry):
@@ -566,8 +636,9 @@
     features = embed_weight.shape[1]
     span = features // cols
     width = in_swapped.shape[1]
-    chunk = min(128, width // 2)
-    chunks = width // 2 // chunk
+    chunk = min(256, width // 2)
+    chunks = 2 * (width // 2 // chunk)
+    half = tokens // 2
     vmem = pl.BlockSpec(memory_space=pltpu.VMEM)
     anywhere = pl.BlockSpec(memory_space=pl.ANY)
     dma = pltpu.SemaphoreType.DMA
@@ -584,20 +655,22 @@
             pltpu.VMEM((2,) + in_swapped.shape, bf16),
             pltpu.VMEM((width, span), bf16),
             pltpu.VMEM((width, span), bf16),
+            pltpu.VMEM((rows, per_row, 128), f32),
             pltpu.VMEM((2, tokens, span), f32),
-            pltpu.VMEM((2, tokens, span), bf16),
-            pltpu.VMEM((2, 2, tokens, chunk), f32),
-            pltpu.VMEM((2, chunks, tokens, chunk), bf16),
-            pltpu.VMEM((2, chunks, tokens, chunk), bf16),
-            pltpu.VMEM((2, chunks, tokens, chunk), bf16),
-            pltpu.VMEM((2, tokens, span), f32),
-            pltpu.VMEM((rows, per_row, span), bf16),
-            pltpu.VMEM((rows, per_row, span), bf16),
-            pltpu.VMEM((rows, per_row, span), bf16),
-            pltpu.VMEM((rows, per_row, span), bf16),
+            pltpu.VMEM((2, 2, half, span), bf16),
+            pltpu.VMEM((2, chunks, half, chunk), bf16),
+            pltpu.VMEM((2, chunks, half, chunk), bf16),
+            pltpu.VMEM((2, chunks, half, chunk), bf16),
+            pltpu.VMEM((2, 2, half, span), f32),
+            pltpu.VMEM((2, half, span), bf16),
+            pltpu.VMEM((2, half, span), bf16),
+            pltpu.VMEM((2, rows, per_row // 2, span), bf16),
+            pltpu.VMEM((2, rows, per_row // 2, span), bf16),
             dma((4,)),
             dma((cols,)),
             dma((cols,)),
+            dma((rows,)),
+            dma((rows,)),
             dma((rows,)),
             dma((rows,)),
             dma((2, chunks)),
@@ -605,10 +678,10 @@
             dma((2, chunks)),
             dma((2, chunks)),
             dma((2,)),
-            dma((rows,)),
-            dma((rows,)),
-            dma((rows,)),
-            dma((rows,)),
+            dma((2,)),
+            dma((2,)),
+            dma((2, rows)),
+            dma((2, rows)),
         ],
         compiler_params=pltpu.CompilerParams(
             collective_id=1, has_side_effects=True, vmem_limit_bytes=56 * MIB
@@ -617,13 +690,6 @@
             flops=10_000_000_000, bytes_accessed=30_000_000, transcendentals=0
         ),
     )(patches, embed_weight, embed_bias, mlp_in, in_swapped, mlp_out)
-
-
-def to_planes(field):
-    moved = jnp.pad(
-        field.transpose(0, 3, 1, 2), ((0, 0), (0, 5), (0, WIDE - SIDE), (0, WIDE - SIDE))
-    )
-    return moved.reshape(field.shape[0], 8, WIDE * WIDE)
 
 
 def on_device(
@@ -642,26 +708,22 @@
 ):
     rows = lax.axis_size("row")
     cols = lax.axis_size("col")
-    depth = stem_weight.shape[1]
-    stem = jnp.pad(stem_weight.reshape(9, 3, depth), ((0, 7), (0, 5), (0, 0))).reshape(128, depth)
-    out_t = jnp.pad(out_weight.T, ((0, 13), (0, 0)))
-    planes, in_swapped = run_score(
-        to_planes(images),
-        to_planes(noise_field),
-        stem,
+    lines, in_swapped = run_score(
+        images.transpose(1, 3, 0, 2),
+        noise_field.transpose(1, 3, 0, 2),
+        stem_weight,
         level_one,
         down_weight,
         level_two,
         up_weight,
-        out_t,
+        out_weight.T,
         mlp_in,
     )
     count = images.shape[0]
-    planes = planes.reshape(count, 8, WIDE, WIDE)[:, 0:3, 0:SIDE, 0:SIDE]
-    purified = planes.transpose(0, 2, 3, 1)
+    purified = lines.transpose(2, 0, 3, 1)
     grid = SIDE // PATCH
-    patches = planes.astype(bf16).reshape(count, 3, grid, PATCH, grid, PATCH)
-    patches = patches.transpose(0, 2, 4, 3, 5, 1).reshape(count * grid * grid, PATCH * PATCH * 3)
+    patches = lines.astype(bf16).reshape(grid, PATCH, 3, count, grid, PATCH)
+    patches = patches.transpose(3, 0, 4, 1, 5, 2).reshape(count * grid * grid, PATCH * PATCH * 3)
     pixels = patches.shape[1]
     patches = jnp.pad(patches.astype(f32), ((0, 0), (0, -pixels % 128)))
     encoded = run_mlp(

time: 114 us -> 99.8 us (0.88)
  Pallas kernels: 101 us -> 93.8 us
  local copies, waits for them, and re-layouts: 10.6 us -> 3.52 us
    pallas_call x1, Pallas kernels: 81.3 us -> 73.3 us  [run_mlp(): pl.pallas_call(functools.partial(mlp_kernel, rows, cols, chunk), out_shap...]
    reshape x5 -> x0, local copies, waits for them, and re-layouts: 3.87 us -> none  [the longest x2 1.54 us: to_planes(): return moved.reshape(field.shape[0], 8, WIDE * WIDE)]
    unnamed x5 -> x4, local copies, waits for them, and re-layouts: 4.11 us -> 2.18 us
    pad x3 -> x0, local copies, waits for them, and re-layouts: 1.32 us -> none  [the longest x1 1.28 us: on_device(): out_t = jnp.pad(out_weight.T, ((0, 13), (0, 0)))]
where the time goes in v2:
time: 99.8 us; the launch traced here: 99.5 us
  Pallas kernels  93.8 us (94%)
  local copies, waits for them, and re-layouts  3.52 us (4%)
  other arithmetic  1.54 us (2%)
    pallas_call x1, Pallas kernels, run_mlp(): pl.pallas_call(functools.partial(mlp_kernel, rows, cols, chunk), out_shap...  73.3 us
    pallas_call x1, Pallas kernels, run_score(): pl.pallas_call(score_kernel, out_shape=(jax.ShapeDtypeStruct(images.shape...  20.5 us
    unnamed x4, local copies, waits for them, and re-layouts  2.18 us

profile of v2, /device:TPU:0, one launch (start us, length us, event | category | flops | bytes accessed | tf_op | source)
XLA Modules:
  0.0 99.5 jit_solution(5625756693505495055)
XLA Ops:
  0.6 20.5 %shard_map.131 = (f32[28,3,2,28]{3,2,1,0:T(2,128)}, bf16[768,3072]{1,0:T(8,128)(2,1)}) custom-call(f32[28,3,2,28]{3,2,1,0:T(2,128)} %bitcast.8, f32[28,3,2,28]{3,2,1,0:T(2,128)} %bitcast.9, bf16[27,256]{1,0:T(8,128)(2,1)} %stem_weight.1, bf16[4,2304,256]{2,1,0:T(8,128)(2,1)} %level_one_hbm.1, bf16[1024,256]{1,0:T(8,128)(2,1)} %down_hbm.1, ...), custom_call_target="tpu_custom_call" | custom-call | flops 10000000000 | bytes 30000000 | tf_op jit(solution)/shard_map/pallas_call | solution.py:251
  21.1 0.9 convert_element_type.15
  22.0 0.1 convert_element_type.16
  22.1 0.8 copy.15
  22.9 0.4 convert_element_type.18
  23.4 0.6 pad_convert_fusion.patches
  24.0 0.0 copy-start
  24.0 73.3 %shard_map.132 = bf16[64,768]{1,0:T(8,128)(2,1)} custom-call(f32[8,640]{1,0:T(8,128)} %pad_convert_fusion.patches, bf16[588,6144]{1,0:T(8,128)(2,1)} %embed_weight.1, f32[1,6144]{1,0:T(1,128)} %bitcast.10, bf16[768,6144]{1,0:T(8,128)(2,1)} %mlp_in.3, bf16[768,3072]{1,0:T(8,128)(2,1)} %get-tuple-element.5.in_swapped, bf16[6144,768]{1,0:T(8,128)(2,1)} %mlp_out.1), custom_call_target="tpu_custom_call" | custom-call | flops 10000000000 | bytes 30000000 | tf_op jit(solution)/shard_map/pallas_call | solution.py:645
  97.3 0.0 copy-done
  97.4 0.6 copy.18
  98.0 1.5 %copy.19 = bf16[64,768]{1,0:T(8,128)(2,1)} copy(bf16[64,768]{1,0:T(8,128)(2,1)} %shard_map.132) | data formatting | bytes 196608
Async XLA Ops:
  24.0 73.3 %copy-start = (f32[28,3,2,28]{3,2,1,0:T(2,128)S(1)}, f32[28,3,2,28]{3,2,1,0:T(2,128)}, u32[]{:S(2)}) copy-start(f32[28,3,2,28]{3,2,1,0:T(2,128)} %get-tuple-element.4) | copy-start | bytes 56452

commit v3 on v2

--- a/solution.py
+++ b/solution.py
@@ -40,7 +40,7 @@
 
 
 def masked_act(stream, wide, side):
-    column = lax.broadcasted_iota(jnp.int32, stream.shape, 0) % wide
+    column = lax.broadcasted_iota(jnp.int32, stream.shape, 0) & (wide - 1)
     return jnp.where(column < side, jax.nn.gelu(stream), 0.0)
 
 
@@ -54,15 +54,10 @@
 
 
 def conv_rows(field, weight, at, rows, wide):
-    span = weight.shape[0] // 3
-    total = None
-    for row_off in range(3):
-        part = dot(
-            field[at + row_off * wide : at + row_off * wide + rows, :],
-            weight[row_off * span : (row_off + 1) * span, :],
-        )
-        total = part if total is None else total + part
-    return total
+    around = [
+        field[at + row_off * wide : at + row_off * wide + rows, :] for row_off in range(3)
+    ]
+    return dot(jnp.concatenate(around, axis=1), weight[...])
 
 
 def score_kernel(
@@ -133,7 +128,7 @@
         stem[8 * g : 8 * g + 3, :] = stem_rows[3 * g : 3 * g + 3, :]
     cells = SIDE * WIDE
     ccells = HALF * HWIDE
-    tile = 7 * WIDE
+    tile = HALF * WIDE
     for field, row, last in (
         (field_a, WIDE, cells),
         (field_b, WIDE, cells),
@@ -305,6 +300,7 @@
     statistics,
     values,
     normed,
+    mine,
     partial_out,
     partial_in,
     hidden,
@@ -550,18 +546,23 @@
             def _():
                 half = i // per_half
                 at = pl.multiple_of((d * per_half + i % per_half) * chunk, chunk)
-                mine = dot(normed[0, half], w_in[0, :, pl.ds(at, chunk)]) + dot(
-                    normed[1, half], w_in[1, :, pl.ds(at, chunk)]
-                )
+
+                @pl.when(half == 0)
+                def _():
+                    both = dot(
+                        normed[0].reshape(tokens, span), w_in[0, :, pl.ds(at, chunk)]
+                    ) + dot(normed[1].reshape(tokens, span), w_in[1, :, pl.ds(at, chunk)])
+                    mine[d, i] = both[0 : tokens // 2]
+                    mine[d, i + per_half] = both[tokens // 2 :]
 
                 @pl.when(place[d] == 0)
                 def _():
-                    partial_out[d, i] = mine.astype(bf16)
+                    partial_out[d, i] = mine[d, i].astype(bf16)
 
                 @pl.when(place[d] > 0)
                 def _():
                     rs_copy(d, i).wait_recv()
-                    whole = mine + partial_in[d, i].astype(f32)
+                    whole = mine[d, i] + partial_in[d, i].astype(f32)
 
                     @pl.when(place[d] < last)
                     def _():
@@ -658,6 +659,7 @@
             pltpu.VMEM((rows, per_row, 128), f32),
             pltpu.VMEM((2, tokens, span), f32),
             pltpu.VMEM((2, 2, half, span), bf16),
+            pltpu.VMEM((2, chunks, half, chunk), f32),
             pltpu.VMEM((2, chunks, half, chunk), bf16),
             pltpu.VMEM((2, chunks, half, chunk), bf16),
             pltpu.VMEM((2, chunks, half, chunk), bf16),

time: 99.8 us -> 100 us (level)
  no operation moved by 1% of the time
where the time goes in v3:
time: 100 us
  Pallas kernels  94.3 us (94%)
  local copies, waits for them, and re-layouts  3.52 us (4%)
  other arithmetic  1.54 us (2%)
    pallas_call x1, Pallas kernels, run_mlp(): pl.pallas_call(functools.partial(mlp_kernel, rows, cols, chunk), out_shap...  73.1 us
    pallas_call x1, Pallas kernels, run_score(): pl.pallas_call(score_kernel, out_shape=(jax.ShapeDtypeStruct(images.shape...  21.2 us
    unnamed x4, local copies, waits for them, and re-layouts  2.18 us

profile of v3, /device:TPU:0, one launch (start us, length us, event | category | flops | bytes accessed | tf_op | source)
XLA Modules:
  0.0 100.0 jit_solution(2147303914771001496)
XLA Ops:
  0.6 21.2 %shard_map.131 = (f32[28,3,2,28]{3,2,1,0:T(2,128)}, bf16[768,3072]{1,0:T(8,128)(2,1)}) custom-call(f32[28,3,2,28]{3,2,1,0:T(2,128)} %bitcast.8, f32[28,3,2,28]{3,2,1,0:T(2,128)} %bitcast.9, bf16[27,256]{1,0:T(8,128)(2,1)} %stem_weight.1, bf16[4,2304,256]{2,1,0:T(8,128)(2,1)} %level_one_hbm.1, bf16[1024,256]{1,0:T(8,128)(2,1)} %down_hbm.1, ...), custom_call_target="tpu_custom_call" | custom-call | flops 10000000000 | bytes 30000000 | tf_op jit(solution)/shard_map/pallas_call | solution.py:246
  21.8 0.9 convert_element_type.15
  22.7 0.1 convert_element_type.16
  22.8 0.8 copy.15
  23.6 0.4 convert_element_type.18
  24.1 0.6 pad_convert_fusion.patches
  24.7 0.0 copy-start
  24.7 73.1 %shard_map.132 = bf16[64,768]{1,0:T(8,128)(2,1)} custom-call(f32[8,640]{1,0:T(8,128)} %pad_convert_fusion.patches, bf16[588,6144]{1,0:T(8,128)(2,1)} %embed_weight.1, f32[1,6144]{1,0:T(1,128)} %bitcast.10, bf16[768,6144]{1,0:T(8,128)(2,1)} %mlp_in.3, bf16[768,3072]{1,0:T(8,128)(2,1)} %get-tuple-element.5.in_swapped, bf16[6144,768]{1,0:T(8,128)(2,1)} %mlp_out.1), custom_call_target="tpu_custom_call" | custom-call | flops 10000000000 | bytes 30000000 | tf_op jit(solution)/shard_map/pallas_call | solution.py:646
  97.8 0.0 copy-done
  97.8 0.6 copy.18
  98.5 1.5 %copy.19 = bf16[64,768]{1,0:T(8,128)(2,1)} copy(bf16[64,768]{1,0:T(8,128)(2,1)} %shard_map.132) | data formatting | bytes 196608
Async XLA Ops:
  24.7 73.1 %copy-start = (f32[28,3,2,28]{3,2,1,0:T(2,128)S(1)}, f32[28,3,2,28]{3,2,1,0:T(2,128)}, u32[]{:S(2)}) copy-start(f32[28,3,2,28]{3,2,1,0:T(2,128)} %get-tuple-element.4) | copy-start | bytes 56452

commit v4 on v2

--- a/solution.py
+++ b/solution.py
@@ -17,7 +17,7 @@
 step_size = 0.25
 noise_gain = math.sqrt(0.5)
 ln_epsilon = 1e-06
-LAG = 2
+LAG = 3
 MESH = pl.DeviceIdType.MESH
 MIB = 1024 * 1024
 f32 = jnp.float32

time: 99.8 us -> 99 us (level)
  no operation moved by 1% of the time
where the time goes in v4:
time: 99 us; the launch traced here: 98.7 us
  Pallas kernels  93 us (94%)
  local copies, waits for them, and re-layouts  3.52 us (4%)
  other arithmetic  1.54 us (2%)
    pallas_call x1, Pallas kernels, run_mlp(): pl.pallas_call(functools.partial(mlp_kernel, rows, cols, chunk), out_shap...  72.5 us
    pallas_call x1, Pallas kernels, run_score(): pl.pallas_call(score_kernel, out_shape=(jax.ShapeDtypeStruct(images.shape...  20.5 us
    unnamed x4, local copies, waits for them, and re-layouts  2.18 us

profile of v4, /device:TPU:0, one launch (start us, length us, event | category | flops | bytes accessed | tf_op | source)
XLA Modules:
  0.0 98.7 jit_solution(7912652501579762651)
XLA Ops:
  0.6 20.5 %shard_map.131 = (f32[28,3,2,28]{3,2,1,0:T(2,128)}, bf16[768,3072]{1,0:T(8,128)(2,1)}) custom-call(f32[28,3,2,28]{3,2,1,0:T(2,128)} %bitcast.8, f32[28,3,2,28]{3,2,1,0:T(2,128)} %bitcast.9, bf16[27,256]{1,0:T(8,128)(2,1)} %stem_weight.1, bf16[4,2304,256]{2,1,0:T(8,128)(2,1)} %level_one_hbm.1, bf16[1024,256]{1,0:T(8,128)(2,1)} %down_hbm.1, ...), custom_call_target="tpu_custom_call" | custom-call | flops 10000000000 | bytes 30000000 | tf_op jit(solution)/shard_map/pallas_call | solution.py:251
  21.1 0.9 convert_element_type.15
  22.0 0.1 convert_element_type.16
  22.1 0.8 copy.15
  22.9 0.4 convert_element_type.18
  23.4 0.6 pad_convert_fusion.patches
  24.0 0.0 copy-start
  24.0 72.5 %shard_map.132 = bf16[64,768]{1,0:T(8,128)(2,1)} custom-call(f32[8,640]{1,0:T(8,128)} %pad_convert_fusion.patches, bf16[588,6144]{1,0:T(8,128)(2,1)} %embed_weight.1, f32[1,6144]{1,0:T(1,128)} %bitcast.10, bf16[768,6144]{1,0:T(8,128)(2,1)} %mlp_in.3, bf16[768,3072]{1,0:T(8,128)(2,1)} %get-tuple-element.5.in_swapped, bf16[6144,768]{1,0:T(8,128)(2,1)} %mlp_out.1), custom_call_target="tpu_custom_call" | custom-call | flops 10000000000 | bytes 30000000 | tf_op jit(solution)/shard_map/pallas_call | solution.py:645
  96.5 0.0 copy-done
  96.5 0.6 copy.18
  97.2 1.5 %copy.19 = bf16[64,768]{1,0:T(8,128)(2,1)} copy(bf16[64,768]{1,0:T(8,128)(2,1)} %shard_map.132) | data formatting | bytes 196608
Async XLA Ops:
  24.0 72.5 %copy-start = (f32[28,3,2,28]{3,2,1,0:T(2,128)S(1)}, f32[28,3,2,28]{3,2,1,0:T(2,128)}, u32[]{:S(2)}) copy-start(f32[28,3,2,28]{3,2,1,0:T(2,128)} %get-tuple-element.4) | copy-start | bytes 56452
